TPU v7x, 32 devices: a whole 2x2x4 slice. The times are simulated.
32 devices in a mesh: ctx: 8 (over z, core), tp: 4 (over y, x).
Axes of the slice: x: 2, y: 2, z: 4, core: 2. Of those that a mesh axis runs over, the one named last changes fastest.
Arguments:
- queries: bfloat16 [512, 4096], P('ctx', 'tp'), may hold values from -6 to 6
- keys: bfloat16 [512, 256], P('ctx'), may hold values from -6 to 6
- values: bfloat16 [512, 256], P('ctx'), may hold values from -6 to 6
- resid: bfloat16 [512, 4096], P(('ctx', 'tp')), may hold values from -4 to 4
- out_proj: bfloat16 [4096, 4096], P('tp'), may hold values from -0.375 to 0.375
- norm_gain: float32 [4096], replicated, may hold values from 0.1 to 1.9
- expert_ids: int32 [512, 8], P(('ctx', 'tp')), may hold values from 0 to 15, all different within a row; in each aligned block of 16 rows (0 to 15, 16 to 31, ...) at most 10 rows name the same one
- gates: float32 [512, 8], P(('ctx', 'tp')), may hold values from 0.1 to 0.5
- w_gate: bfloat16 [16, 1536, 4096], P('ctx', 'tp'), may hold values from -0.09375 to 0.09375
- w_up: bfloat16 [16, 1536, 4096], P('ctx', 'tp'), may hold values from -0.09375 to 0.09375
- w_down: bfloat16 [16, 1536, 4096], P('ctx', 'tp'), may hold values from -0.15625 to 0.15625
- cotangent: bfloat16 [512, 4096], P(('ctx', 'tp')), may hold values from -2 to 2
Outputs:
- layer_out: bfloat16 [512, 4096], P(('ctx', 'tp'))
- grad_gate: bfloat16 [16, 1536, 4096], P('ctx', 'tp')
- grad_up: bfloat16 [16, 1536, 4096], P('ctx', 'tp')
- grad_down: bfloat16 [16, 1536, 4096], P('ctx', 'tp')
Inputs may be any that keep to these rules, and one draw needn't show every extreme that they name: `expert_ids`: in the 16 rows of one device (aligned blocks of rows) no expert is named more than 10 times, a bound that some block reaches; each row names 8 different experts.
All inputs are finite; a program needn't handle non-finite values.
Results may differ from a plain program's by a relative error of at most 0.025.
Values may be sent and summed in bfloat16 or wider, within the bound.
A program may use at most 192 MiB of HBM per device.

v0:
```python
import math

import jax
import jax.numpy as jnp
from jax import lax
from jax.sharding import PartitionSpec as P

D = 4096
QHEADS = 32
KVHEADS = 2
HEAD = 128
TOPK = 8


def shards(
    queries,
    keys,
    values,
    resid,
    out_proj,
    norm_gain,
    expert_ids,
    gates,
    w_gate,
    w_up,
    w_down,
    cotangent,
):
    groups = lax.axis_size("ctx")
    tensor = lax.axis_size("tp")
    tok_ctx = queries.shape[0]
    heads_dev = queries.shape[1] // HEAD
    group_size = QHEADS // KVHEADS
    kv_head = lax.axis_index("tp") * heads_dev // group_size
    key_mine = lax.dynamic_slice_in_dim(keys, kv_head * HEAD, HEAD, 1)
    value_mine = lax.dynamic_slice_in_dim(values, kv_head * HEAD, HEAD, 1)
    query_pos = lax.axis_index("ctx") * tok_ctx + jnp.arange(tok_ctx, dtype=jnp.int32)
    query_heads = queries.reshape(tok_ctx, heads_dev, HEAD)
    score_scale = 1.0 / math.sqrt(HEAD)
    running = jnp.full((heads_dev, tok_ctx), -1e30, jnp.float32)
    key_piece = lax.all_gather(key_mine, "ctx", axis=0, tiled=True)
    value_piece = lax.all_gather(value_mine, "ctx", axis=0, tiled=True)
    scores = (
        jnp.einsum("qhd,kd->hqk", query_heads, key_piece, preferred_element_type=jnp.float32)
        * score_scale
    )
    key_pos = jnp.arange(key_piece.shape[0], dtype=jnp.int32)
    visible = key_pos[None, None, :] <= query_pos[None, :, None]
    block_max = jnp.max(jnp.where(visible, scores, -1e30), axis=2)
    new_running = jnp.maximum(running, block_max)
    weights = jnp.where(visible, jnp.exp(scores - new_running[:, :, None]), 0.0)
    denom = jnp.sum(weights, axis=2)
    accumulated = jnp.einsum(
        "hqk,kd->hqd", weights.astype(jnp.bfloat16), value_piece, preferred_element_type=jnp.float32
    )
    attn_heads = (accumulated / denom[:, :, None]).astype(jnp.bfloat16)
    attn = jnp.transpose(attn_heads, (1, 0, 2)).reshape(tok_ctx, heads_dev * HEAD)
    row_total = resid.shape[0]
    head_mix = lax.psum_scatter(
        jnp.dot(attn, out_proj, preferred_element_type=jnp.float32).astype(jnp.bfloat16),
        "tp",
        scatter_dimension=0,
        tiled=True,
    ).astype(jnp.float32)
    stream = resid.astype(jnp.float32) + head_mix
    normed = (
        stream * lax.rsqrt(jnp.mean(stream * stream, axis=1, keepdims=True) + 1e-06) * norm_gain
    ).astype(jnp.bfloat16)
    exp_dev = w_gate.shape[0]
    experts_all = exp_dev * groups
    capacity = 5 * row_total * TOPK // (4 * experts_all)
    slot_total = experts_all * capacity
    flat_ids = expert_ids.reshape(-1)
    pick_table = (flat_ids[:, None] == jnp.arange(experts_all, dtype=jnp.int32)[None, :]).astype(
        jnp.int32
    )
    before = jnp.cumsum(pick_table, axis=0) - pick_table
    rank_in = jnp.sum(before * pick_table, axis=1)
    owner_group = flat_ids // exp_dev
    local_exp = flat_ids % exp_dev
    target = (local_exp * groups + owner_group) * capacity + rank_in
    placement = (target[:, None] == jnp.arange(slot_total, dtype=jnp.int32)[None, :]).astype(
        jnp.float32
    )
    placement = placement.reshape(row_total, TOPK, slot_total)
    hit_table = jnp.sum(placement, axis=1)
    weighted = jnp.sum(placement * gates[:, :, None], axis=1)
    send_rows = jnp.einsum(
        "rs,rd->sd", hit_table.astype(jnp.bfloat16), normed, preferred_element_type=jnp.float32
    ).astype(jnp.bfloat16)
    send_grads = jnp.einsum(
        "rs,rd->sd", weighted, cotangent.astype(jnp.float32), precision=lax.Precision.HIGHEST
    ).astype(jnp.bfloat16)
    send_rows = send_rows.reshape(exp_dev, groups, capacity, D)
    send_grads = send_grads.reshape(exp_dev, groups, capacity, D)

    def spread_out(block_in):
        widened = jnp.broadcast_to(block_in[:, :, None], (exp_dev, groups, tensor, capacity, D))
        return widened.reshape(exp_dev, groups * tensor, capacity, D)

    rows_in, grads_in = (
        lax.all_to_all(
            spread_out(send_rows), ("ctx", "tp"), split_axis=1, concat_axis=1, tiled=True
        ),
        lax.all_to_all(
            spread_out(send_grads), ("ctx", "tp"), split_axis=1, concat_axis=1, tiled=True
        ),
    )
    expert_rows = rows_in.reshape(exp_dev, -1, D)
    expert_grads = grads_in.reshape(exp_dev, -1, D)
    gate_val = jnp.einsum("end,efd->enf", expert_rows, w_gate, preferred_element_type=jnp.float32)
    up_val = jnp.einsum("end,efd->enf", expert_rows, w_up, preferred_element_type=jnp.float32)
    sigmoid_val = jax.nn.sigmoid(gate_val)
    silu_val = gate_val * sigmoid_val
    activated = (silu_val * up_val).astype(jnp.bfloat16)
    partial_value = jnp.einsum(
        "enf,efd->end", activated, w_down, preferred_element_type=jnp.float32
    )
    partial_value = partial_value.astype(jnp.bfloat16).reshape(rows_in.shape)
    back_act = jnp.einsum("end,efd->enf", expert_grads, w_down, preferred_element_type=jnp.float32)
    d_gate = (back_act * up_val * sigmoid_val * (1.0 + gate_val * (1.0 - sigmoid_val))).astype(
        jnp.bfloat16
    )
    d_up = (back_act * silu_val).astype(jnp.bfloat16)
    grad_down = jnp.einsum(
        "enf,end->efd", activated, expert_grads, preferred_element_type=jnp.float32
    )
    grad_gate = jnp.einsum("enf,end->efd", d_gate, expert_rows, preferred_element_type=jnp.float32)
    grad_up = jnp.einsum("enf,end->efd", d_up, expert_rows, preferred_element_type=jnp.float32)
    partial_value, grad_outs = (
        partial_value,
        (
            grad_gate.astype(jnp.bfloat16),
            grad_up.astype(jnp.bfloat16),
            grad_down.astype(jnp.bfloat16),
        ),
    )
    returned = lax.all_to_all(partial_value, ("ctx", "tp"), split_axis=1, concat_axis=1, tiled=True)
    returned = returned.reshape(exp_dev, groups, tensor, capacity, D).astype(jnp.float32)
    result = jnp.sum(returned, axis=2).astype(jnp.bfloat16)
    combined = jnp.einsum(
        "rs,sd->rd",
        weighted,
        result.reshape(slot_total, D).astype(jnp.float32),
        precision=lax.Precision.HIGHEST,
    )
    layer_out = (stream + combined).astype(jnp.bfloat16)
    return (layer_out, grad_outs[0], grad_outs[1], grad_outs[2])


def solution(mesh):
    in_specs = (
        P("ctx", "tp"),
        P("ctx", None),
        P("ctx", None),
        P(("ctx", "tp"), None),
        P("tp", None),
        P(),
        P(("ctx", "tp"), None),
        P(("ctx", "tp"), None),
        P("ctx", "tp", None),
        P("ctx", "tp", None),
        P("ctx", "tp", None),
        P(("ctx", "tp"), None),
    )
    out_specs = (
        P(("ctx", "tp"), None),
        P("ctx", "tp", None),
        P("ctx", "tp", None),
        P("ctx", "tp", None),
    )
    return jax.shard_map(shards, mesh=mesh, in_specs=in_specs, out_specs=out_specs, check_vma=False)
```

profile of v0, /device:TPU:0, one launch (start us, length us, event | category | flops | bytes accessed | tf_op | source)
XLA Modules:
  0.0 478.7 jit_solution(8300164558124316895)
XLA Ops:
  7.2 0.0 reduce-scatter.2.cloned.1.call-start
  7.2 0.1 iota_compare_fusion.1
  7.4 0.7 constant_dynamic-slice_fusion.1
  8.1 15.7 %all_gather.6 = bf16[512,128]{1,0:T(8,128)(2,1)S(1)} all-gather(bf16[64,128]{1,0:T(8,128)(2,1)S(1)} %constant_dynamic-slice_fusion.1), channel_id=1, replica_groups=mesh['ctx'=8,'tp'=4] {'ctx'}, dimensions={0}, use_global_device_ids=true | all-gather | bytes 147456 | tf_op jit(solution)/shard_map/all_gather | solution.py:41
  23.8 1.3 select_reduce_fusion
  25.1 0.7 constant_dynamic-slice_fusion
  25.8 14.0 %all_gather.7 = bf16[512,128]{1,0:T(8,128)(2,1)S(1)} all-gather(bf16[64,128]{1,0:T(8,128)(2,1)S(1)} %constant_dynamic-slice_fusion), channel_id=1, replica_groups=mesh['ctx'=8,'tp'=4] {'ctx'}, dimensions={0}, use_global_device_ids=true | all-gather | bytes 147456 | tf_op jit(solution)/shard_map/all_gather | solution.py:42
  39.8 0.3 fusion.15
  40.1 0.4 fusion.13
  40.5 5.8 %convolution_convert_fusion.6 = bf16[64,4096]{1,0:T(8,128)(2,1)} fusion(bf16[1024,4096]{1,0:T(8,128)(2,1)} %param.16, bf16[8,8,8,128]{3,2,1,0:T(8,128)(2,1)S(1)} %fusion.13), kind=kOutput, calls=%fused_computation.10 | convolution fusion | flops 537133056 | bytes 9043968 | tf_op jit(solution)/shard_map/dot_general | solution.py:60
  46.4 0.0 reduce-scatter.2.cloned.1.call-update
  46.4 0.1 copy.60
  46.5 0.1 eq.31
  46.6 0.1 fusion.31
  46.7 0.2 reduce_window_sum.11
  46.8 0.2 select_reduce_fusion.2
  47.0 0.1 reduce_sum.61
  47.1 0.0 copy-done.5
  47.1 0.1 copy.65
  47.2 0.2 convert_reduce_fusion
  47.4 24.9 %reduce-scatter.2.cloned.1.call-done = bf16[16,4096]{1,0:T(8,128)(2,1)} async-done(((bf16[64,4096]{1,0:T(8,128)(2,1)}), bf16[16,4096]{1,0:T(8,128)(2,1)}) %reduce-scatter.2.cloned.1.call-update) | async-done | bytes 131088 | tf_op jit(solution)/shard_map/reduce_scatter | solution.py:59
  72.3 1.1 multiply_reduce_fusion
  73.4 1.4 convolution_convert_fusion.5
  74.8 0.5 broadcast_in_dim.49
  75.3 1.4 copy.66
  76.7 5.6 %broadcast_in_dim.50 = bf16[2,8,4,10,4096]{4,0,3,2,1:T(2,128)(2,1)} broadcast(bf16[2,8,10,4096]{3,0,2,1:T(2,128)(2,1)S(1)} %copy.66), dimensions={0,1,3,4} | broadcast | bytes 6553600 | tf_op jit(solution)/shard_map/broadcast_in_dim | solution.py:98
  82.4 4.7 all-to-all-start
  87.1 1.2 convolution_convert_fusion.4
  88.3 0.5 broadcast_in_dim.51
  88.8 1.4 copy.71
  90.2 114.6 %all-to-all-done = bf16[2,32,10,4096]{3,0,2,1:T(2,128)(2,1)} async-done(((bf16[2,32,10,4096]{3,0,2,1:T(2,128)(2,1)}), bf16[2,32,10,4096]{3,0,2,1:T(2,128)(2,1)}, u32[]{:S(2)}, u32[]{:S(2)}) %all-to-all-start) | async-done | bytes 5242912 | tf_op jit(solution)/shard_map/all_to_all | solution.py:102
  204.7 5.6 %broadcast_in_dim.52 = bf16[2,8,4,10,4096]{4,0,3,2,1:T(2,128)(2,1)} broadcast(bf16[2,8,10,4096]{3,0,2,1:T(2,128)(2,1)S(1)} %copy.71), dimensions={0,1,3,4} | broadcast | bytes 6553600 | tf_op jit(solution)/shard_map/broadcast_in_dim | solution.py:98
  210.3 6.4 %all-to-all-start.2 = ((bf16[2,32,10,4096]{3,0,2,1:T(2,128)(2,1)}), bf16[2,32,10,4096]{3,0,2,1:T(2,128)(2,1)}, u32[]{:S(2)}, u32[]{:S(2)}) async-start(bf16[2,32,10,4096]{3,0,2,1:T(2,128)(2,1)} %bitcast.53), calls=%async_computation.3 | async-start | bytes 10485760 | tf_op jit(solution)/shard_map/all_to_all | solution.py:105
  216.7 12.4 %fusion.8 = f32[2,320,384]{2,1,0:T(8,128)S(1)} fusion(bf16[2,384,4096]{2,1,0:T(8,128)(2,1)} %param.20, bf16[2,320,4096]{2,0,1:T(2,128)(2,1)} %bitcast.6), kind=kOutput, calls=%fused_computation.17 | convolution fusion | flops 2013265920 | bytes 12517376 | tf_op jit(solution)/shard_map/end,efd->enf/dot_general | solution.py:111
  229.1 12.4 %multiply_convert_fusion.2 = (bf16[2,320,384]{2,1,0:T(8,128)(2,1)S(1)}, f32[2,320,384]{2,1,0:T(8,128)S(1)}) fusion(f32[2,320,384]{2,1,0:T(8,128)S(1)} %fusion.8, bf16[2,384,4096]{2,1,0:T(8,128)(2,1)} %param.21, bf16[2,320,4096]{2,0,1:T(2,128)(2,1)} %bitcast.6), kind=kOutput, calls=%fused_computation.29 | convolution fusion | flops 2014740480 | bytes 13991936 | tf_op jit(solution)/shard_map/end,efd->enf/dot_general | solution.py:112
  241.6 4.8 %convolution_convert_fusion.3 = bf16[2,320,4096]{2,1,0:T(8,128)(2,1)} fusion(bf16[2,320,384]{2,1,0:T(8,128)(2,1)S(1)} %get-tuple-element.8, bf16[2,384,4096]{2,1,0:T(8,128)(2,1)S(1)} %bitcast.56), kind=kOutput, calls=%fused_computation.3 | convolution fusion | flops 2015887360 | bytes 12025856 | tf_op jit(solution)/shard_map/enf,efd->end/dot_general | solution.py:116
  246.4 10.4 %copy.69 = bf16[2,320,4096]{2,0,1:T(2,128)(2,1)} copy(bf16[2,320,4096]{2,1,0:T(8,128)(2,1)} %convolution_convert_fusion.3) | data formatting | bytes 10485760 | tf_op jit(solution)/shard_map/convert_element_type | solution.py:119
  256.8 77.7 %all-to-all-done.2 = bf16[2,32,10,4096]{3,0,2,1:T(2,128)(2,1)} async-done(((bf16[2,32,10,4096]{3,0,2,1:T(2,128)(2,1)}), bf16[2,32,10,4096]{3,0,2,1:T(2,128)(2,1)}, u32[]{:S(2)}, u32[]{:S(2)}) %all-to-all-start.2) | async-done | bytes 5242912 | tf_op jit(solution)/shard_map/all_to_all | solution.py:105
  334.4 5.8 %all-to-all-start.1 = ((bf16[2,32,10,4096]{3,0,2,1:T(2,128)(2,1)}), bf16[2,32,10,4096]{3,0,2,1:T(2,128)(2,1)}, u32[]{:S(2)}, u32[]{:S(2)}) async-start(bf16[2,32,10,4096]{3,0,2,1:T(2,128)(2,1)} %bitcast.52), calls=%async_computation.2 | async-start | bytes 10485760 | tf_op jit(solution)/shard_map/all_to_all | solution.py:138
  340.3 12.4 %fusion.1 = f32[2,320,384]{2,1,0:T(8,128)S(1)} fusion(bf16[2,384,4096]{2,1,0:T(8,128)(2,1)} %param.22, bf16[2,320,4096]{2,0,1:T(2,128)(2,1)} %bitcast.10), kind=kOutput, calls=%fused_computation.8 | convolution fusion | flops 2013265920 | bytes 12517376 | tf_op jit(solution)/shard_map/end,efd->enf/dot_general | solution.py:120
  352.7 12.2 %convolution_convert_fusion = bf16[2,384,4096]{2,1,0:T(8,128)(2,1)} fusion(bf16[2,320,384]{2,1,0:T(8,128)(2,1)S(1)} %get-tuple-element.8, bf16[2,320,4096]{2,0,1:T(2,128)(2,1)} %bitcast.10), kind=kOutput, calls=%fused_computation | convolution fusion | flops 2016411648 | bytes 12025856 | tf_op jit(solution)/shard_map/enf,end->efd/dot_general | solution.py:125
  364.9 12.8 %convolution_convert_fusion.1 = bf16[2,384,4096]{2,1,0:T(8,128)(2,1)} fusion(bf16[2,320,4096]{2,0,1:T(2,128)(2,1)} %bitcast.6, f32[2,320,384]{2,1,0:T(8,128)S(1)} %fusion.1, f32[2,320,384]{2,1,0:T(8,128)S(1)} %fusion.8), kind=kOutput, calls=%fused_computation.1 | convolution fusion | flops 2017886208 | bytes 13500416 | tf_op jit(solution)/shard_map/enf,end->efd/dot_general | solution.py:129
  377.7 12.5 %convolution_convert_fusion.2 = bf16[2,384,4096]{2,1,0:T(8,128)(2,1)} fusion(bf16[2,320,4096]{2,0,1:T(2,128)(2,1)} %bitcast.6, f32[2,320,384]{2,1,0:T(8,128)S(1)} %fusion.8, f32[2,320,384]{2,1,0:T(8,128)S(1)} %fusion.1, f32[2,320,384]{2,1,0:T(8,128)S(1)} %get-tuple-element.9), kind=kOutput, calls=%fused_computation.2 | convolution fusion | flops 2018869248 | bytes 14483456 | tf_op jit(solution)/shard_map/enf,end->efd/dot_general | solution.py:128
  390.2 67.7 %all-to-all-done.1 = bf16[2,32,10,4096]{3,0,2,1:T(2,128)(2,1)} async-done(((bf16[2,32,10,4096]{3,0,2,1:T(2,128)(2,1)}), bf16[2,32,10,4096]{3,0,2,1:T(2,128)(2,1)}, u32[]{:S(2)}, u32[]{:S(2)}) %all-to-all-start.1) | async-done | bytes 5242912 | tf_op jit(solution)/shard_map/all_to_all | solution.py:138
  457.9 10.1 %bitcast_reduce_fusion = bf16[2,8,10,4096]{3,0,2,1:T(2,128)(2,1)S(1)} fusion(bf16[2,32,10,4096]{3,0,2,1:T(2,128)(2,1)} %all-to-all-done.1), kind=kLoop, calls=%fused_computation.4 | loop fusion | flops 1966080 | bytes 6553600 | tf_op jit(solution)/shard_map/reduce_sum | solution.py:140
  468.0 0.9 copy.70
  468.9 0.5 reshape.143
  469.5 2.3 fusion.3
  (20 shorter events, 0.1 us)
Async XLA Ops:
  7.2 79.9 %copy-start = (bf16[16,4096]{1,0:T(8,128)(2,1)S(1)}, bf16[16,4096]{1,0:T(8,128)(2,1)}, u32[]{:S(2)}) copy-start(bf16[16,4096]{1,0:T(8,128)(2,1)} %param.23) | copy-start | bytes 393220
  7.2 65.1 %reduce-scatter.2.cloned.1.call-start = ((), (), s32[]{:S(2)}) async-start(), calls=%async_computation.4 | async-start | bytes 655360 | tf_op jit(solution)/shard_map/reduce_scatter | solution.py:59
  40.5 5.9 %copy-start.4 = (s32[16,8]{0,1:T(8,128)S(1)}, s32[16,8]{0,1:T(8,128)}, u32[]{:S(2)}) copy-start(s32[16,8]{0,1:T(8,128)} %param.18) | copy-start | bytes 1540
  40.5 6.6 %copy-start.5 = (f32[16,8]{0,1:T(8,128)S(1)}, f32[16,8]{0,1:T(8,128)}, u32[]{:S(2)}) copy-start(f32[16,8]{0,1:T(8,128)} %param.19) | copy-start | bytes 1540
  40.5 31.8 %copy-start.2 = (bf16[16,4096]{1,0:T(8,128)(2,1)S(1)}, bf16[16,4096]{1,0:T(8,128)(2,1)}, u32[]{:S(2)}) copy-start(bf16[16,4096]{1,0:T(8,128)(2,1)} %param.15) | copy-start | bytes 393220
  40.5 32.9 %copy-start.3 = (f32[4096]{0:T(1024)S(1)}, f32[4096]{0:T(1024)}, u32[]{:S(2)}) copy-start(f32[4096]{0:T(1024)} %param.17) | copy-start | bytes 49156
  82.4 122.4 %all-to-all-start = ((bf16[2,32,10,4096]{3,0,2,1:T(2,128)(2,1)}), bf16[2,32,10,4096]{3,0,2,1:T(2,128)(2,1)}, u32[]{:S(2)}, u32[]{:S(2)}) async-start(bf16[2,32,10,4096]{3,0,2,1:T(2,128)(2,1)} %bitcast.54), calls=%async_computation.1 | async-start | bytes 10485760 | tf_op jit(solution)/shard_map/all_to_all | solution.py:102
  210.3 124.1 %all-to-all-start.2 = ((bf16[2,32,10,4096]{3,0,2,1:T(2,128)(2,1)}), bf16[2,32,10,4096]{3,0,2,1:T(2,128)(2,1)}, u32[]{:S(2)}, u32[]{:S(2)}) async-start(bf16[2,32,10,4096]{3,0,2,1:T(2,128)(2,1)} %bitcast.53), calls=%async_computation.3 | async-start | bytes 10485760 | tf_op jit(solution)/shard_map/all_to_all | solution.py:105
  216.7 24.8 %slice-start = ((s8[6291456]{0:T(1024)(128)(4,1)}), s8[4194304]{0:T(1024)(128)(4,1)S(1)}, s32[]{:S(2)}) async-start(s8[6291456]{0:T(1024)(128)(4,1)} %bitcast.55), calls=%async_computation.5 | async-start | bytes 8388608
  229.1 12.5 %slice-start.1 = ((s8[6291456]{0:T(1024)(128)(4,1)}), s8[2097152]{0:T(1024)(128)(4,1)S(1)}, s32[]{:S(2)}) async-start(s8[6291456]{0:T(1024)(128)(4,1)} %bitcast.55), calls=%async_computation.6 | async-start | bytes 4194304
  334.4 123.5 %all-to-all-start.1 = ((bf16[2,32,10,4096]{3,0,2,1:T(2,128)(2,1)}), bf16[2,32,10,4096]{3,0,2,1:T(2,128)(2,1)}, u32[]{:S(2)}, u32[]{:S(2)}) async-start(bf16[2,32,10,4096]{3,0,2,1:T(2,128)(2,1)} %bitcast.52), calls=%async_computation.2 | async-start | bytes 10485760 | tf_op jit(solution)/shard_map/all_to_all | solution.py:138
  457.9 13.8 %copy-start.1 = (bf16[16,4096]{1,0:T(8,128)(2,1)S(1)}, bf16[16,4096]{1,0:T(8,128)(2,1)}, u32[]{:S(2)}) copy-start(bf16[16,4096]{1,0:T(8,128)(2,1)} %param.23) | copy-start | bytes 393220
Sparse Core Ops, SparseCore 0:
  46.5 25.7 reduce-scatter.1
where the time goes:
time: 486 us; the launch traced here: 479 us
  waiting for transfers between devices  285 us (59%)
  matrix products  91.9 us (19%)
  blocking collectives  29.7 us (6%)
  local copies, waits for them, and re-layouts  28.6 us (6%)
  starting transfers between devices  17 us (3%)
  between operations  14.5 us (3%)
  other arithmetic  12.2 us (3%)
    all_to_all x1, waiting for transfers between devices, shards(): lax.all_to_all(spread_out(send_rows), ('ctx', 'tp'), split_axis=1, concat...  115 us
    all_to_all x1, waiting for transfers between devices, shards(): lax.all_to_all(spread_out(send_grads), ('ctx', 'tp'), split_axis=1, conca...  77.7 us
    all_to_all x1, waiting for transfers between devices, shards(): lax.all_to_all(partial_value, ('ctx', 'tp'), split_axis=1, concat_axis=1,...  67.7 us
    reduce_scatter x1, waiting for transfers between devices, shards(): lax.psum_scatter(jnp.dot(attn, out_proj, preferred_element_type=jnp.float...  24.9 us
    all_gather x1, blocking collectives, shards(): key_piece = lax.all_gather(key_mine, 'ctx', axis=0, tiled=True)  15.7 us
    broadcast_in_dim x6, local copies, waits for them, and re-layouts, spread_out(): jnp.broadcast_to(block_in[:, :, None], (exp_dev, groups, tensor, capacity...  14.9 us
    all_gather x1, blocking collectives, shards(): value_piece = lax.all_gather(value_mine, 'ctx', axis=0, tiled=True)  14 us
    dot_general x1, matrix products, shards(): jnp.einsum('enf,end->efd', d_up, expert_rows, preferred_element_type=jnp....  12.8 us
  transfers between devices with their start and end apart: 4, of which 4 were waited for; matrix products, arithmetic and copies ran while one was open for 20% of the time, Pallas kernels for 0%

commit v1 on v0

v1 whole, which is shorter than its diff:
```python
import math

import jax
import jax.numpy as jnp
from jax import lax
from jax.sharding import PartitionSpec as P

D = 4096
QHEADS = 32
KVHEADS = 2
HEAD = 128
TOPK = 8


def shards(
    queries,
    keys,
    values,
    resid,
    out_proj,
    norm_gain,
    expert_ids,
    gates,
    w_gate,
    w_up,
    w_down,
    cotangent,
):
    groups = lax.axis_size("ctx")
    tensor = lax.axis_size("tp")
    tok_ctx = queries.shape[0]
    heads_dev = queries.shape[1] // HEAD
    group_size = QHEADS // KVHEADS
    kv_head = lax.axis_index("tp") * heads_dev // group_size
    key_mine = lax.dynamic_slice_in_dim(keys, kv_head * HEAD, HEAD, 1)
    value_mine = lax.dynamic_slice_in_dim(values, kv_head * HEAD, HEAD, 1)
    query_pos = lax.axis_index("ctx") * tok_ctx + jnp.arange(tok_ctx, dtype=jnp.int32)
    query_heads = queries.reshape(tok_ctx, heads_dev, HEAD)
    score_scale = 1.0 / math.sqrt(HEAD)
    running = jnp.full((heads_dev, tok_ctx), -1e30, jnp.float32)
    key_piece = lax.all_gather(key_mine, "ctx", axis=0, tiled=True)
    value_piece = lax.all_gather(value_mine, "ctx", axis=0, tiled=True)
    scores = (
        jnp.einsum("qhd,kd->hqk", query_heads, key_piece, preferred_element_type=jnp.float32)
        * score_scale
    )
    key_pos = jnp.arange(key_piece.shape[0], dtype=jnp.int32)
    visible = key_pos[None, None, :] <= query_pos[None, :, None]
    block_max = jnp.max(jnp.where(visible, scores, -1e30), axis=2)
    new_running = jnp.maximum(running, block_max)
    weights = jnp.where(visible, jnp.exp(scores - new_running[:, :, None]), 0.0)
    denom = jnp.sum(weights, axis=2)
    accumulated = jnp.einsum(
        "hqk,kd->hqd", weights.astype(jnp.bfloat16), value_piece, preferred_element_type=jnp.float32
    )
    attn_heads = (accumulated / denom[:, :, None]).astype(jnp.bfloat16)
    attn = jnp.transpose(attn_heads, (1, 0, 2)).reshape(tok_ctx, heads_dev * HEAD)
    row_total = resid.shape[0]
    head_mix = lax.psum_scatter(
        jnp.dot(attn, out_proj, preferred_element_type=jnp.float32).astype(jnp.bfloat16),
        "tp",
        scatter_dimension=0,
        tiled=True,
    ).astype(jnp.float32)
    stream = resid.astype(jnp.float32) + head_mix
    normed = (
        stream * lax.rsqrt(jnp.mean(stream * stream, axis=1, keepdims=True) + 1e-06) * norm_gain
    ).astype(jnp.bfloat16)
    exp_dev, ff_dev = w_gate.shape[0], w_gate.shape[1]
    experts_all = exp_dev * groups
    hits = expert_ids[:, :, None] == jnp.arange(experts_all, dtype=jnp.int32)[None, None, :]
    weight_rows = jnp.sum(jnp.where(hits, gates[:, :, None], 0.0), axis=1)
    both = ("ctx", "tp")
    weight_all = lax.all_gather(weight_rows, both, axis=0, tiled=True)
    weight_mine = lax.dynamic_slice_in_dim(
        weight_all, lax.axis_index("ctx") * exp_dev, exp_dev, 1
    )
    weight = jnp.repeat(weight_mine, ff_dev, axis=1)
    cot = lax.all_gather(cotangent, both, axis=0, tiled=True)
    rows = lax.all_gather(normed, both, axis=0, tiled=True)
    wide = exp_dev * ff_dev
    gate_w = w_gate.reshape(wide, D)
    up_w = w_up.reshape(wide, D)
    down_w = w_down.reshape(wide, D)
    f32 = jnp.float32
    back_act = jnp.einsum("td,fd->tf", cot, down_w, preferred_element_type=f32) * weight
    gate_val = jnp.einsum("td,fd->tf", rows, gate_w, preferred_element_type=f32)
    up_val = jnp.einsum("td,fd->tf", rows, up_w, preferred_element_type=f32)
    sigmoid_val = jax.nn.sigmoid(gate_val)
    silu_val = gate_val * sigmoid_val
    activated = (silu_val * up_val * weight).astype(jnp.bfloat16)
    partial = jnp.dot(activated, down_w, preferred_element_type=f32).astype(jnp.bfloat16)
    combined = lax.psum_scatter(partial, both, scatter_dimension=0, tiled=True)
    d_gate = (back_act * up_val * sigmoid_val * (1.0 + gate_val * (1.0 - sigmoid_val))).astype(
        jnp.bfloat16
    )
    d_up = (back_act * silu_val).astype(jnp.bfloat16)

    def grad(left, right):
        out = jnp.einsum("tf,td->fd", left, right, preferred_element_type=f32)
        return out.astype(jnp.bfloat16).reshape(exp_dev, ff_dev, D)

    grad_down = grad(activated, cot)
    grad_gate = grad(d_gate, rows)
    grad_up = grad(d_up, rows)
    layer_out = (stream + combined.astype(f32)).astype(jnp.bfloat16)
    return (layer_out, grad_gate, grad_up, grad_down)


def solution(mesh):
    in_specs = (
        P("ctx", "tp"),
        P("ctx", None),
        P("ctx", None),
        P(("ctx", "tp"), None),
        P("tp", None),
        P(),
        P(("ctx", "tp"), None),
        P(("ctx", "tp"), None),
        P("ctx", "tp", None),
        P("ctx", "tp", None),
        P("ctx", "tp", None),
        P(("ctx", "tp"), None),
    )
    out_specs = (
        P(("ctx", "tp"), None),
        P("ctx", "tp", None),
        P("ctx", "tp", None),
        P("ctx", "tp", None),
    )
    return jax.shard_map(shards, mesh=mesh, in_specs=in_specs, out_specs=out_specs, check_vma=False)
```

time: 486 us -> 353 us (0.73); the launches traced: 479 us -> 353 us
  waiting for transfers between devices: 285 us -> 181 us
  blocking collectives: 29.7 us -> 98.6 us
  matrix products: 91.9 us -> 50.6 us
  local copies, waits for them, and re-layouts: 28.6 us -> 3.39 us
  starting transfers between devices: 17 us -> 0.16 us
  other arithmetic: 12.2 us -> 4.88 us
    all_to_all x3 -> x0, waiting for transfers between devices: 260 us -> none  [the longest x1 115 us: shards(): lax.all_to_all(spread_out(send_rows), ('ctx', 'tp'), split_axis=1, concat...]
    reduce_scatter x0 -> x1, waiting for transfers between devices: none -> 118 us  [shards(): combined = lax.psum_scatter(partial, both, scatter_dimension=0, tiled=True)]
    all_gather x0 -> x1, blocking collectives: none -> 69 us  [shards(): weight_all = lax.all_gather(weight_rows, both, axis=0, tiled=True)]
    dot_general x10 -> x7, matrix products: 84.4 us -> 44 us  [the longest x3 16.7 us: grad(): out = jnp.einsum('tf,td->fd', left, right, preferred_element_type=f32)]
    all_gather x0 -> x2, waiting for transfers between devices: none -> 36.2 us  [the longest x1 36.2 us: shards(): cot = lax.all_gather(cotangent, both, axis=0, tiled=True)]
    all_to_all x3 -> x0, starting transfers between devices: 16.9 us -> none  [the longest x1 6.4 us: shards(): lax.all_to_all(spread_out(send_grads), ('ctx', 'tp'), split_axis=1, conca...]
    broadcast_in_dim x6 -> x1, local copies, waits for them, and re-layouts: 14.9 us -> 0.61 us  [shards(): weight = jnp.repeat(weight_mine, ff_dev, axis=1)]
    convert_element_type x1 -> x0, local copies, waits for them, and re-layouts: 10.4 us -> none  [shards(): partial_value = partial_value.astype(jnp.bfloat16).reshape(rows_in.shape)]
  transfers between devices with their start and end apart: 4 -> 4, of which waited for: 4 -> 3; matrix products, arithmetic and copies ran while one was open for 20% -> 13% of each run, Pallas kernels for 0% -> 0%
where the time goes in v1:
time: 353 us
  waiting for transfers between devices  181 us (51%)
  blocking collectives  98.6 us (28%)
  matrix products  50.6 us (14%)
  between operations  14 us (4%)
  other arithmetic  4.88 us (1%)
    reduce_scatter x1, waiting for transfers between devices, shards(): combined = lax.psum_scatter(partial, both, scatter_dimension=0, tiled=True)  118 us
    all_gather x1, blocking collectives, shards(): weight_all = lax.all_gather(weight_rows, both, axis=0, tiled=True)  69 us
    all_gather x1, waiting for transfers between devices, shards(): cot = lax.all_gather(cotangent, both, axis=0, tiled=True)  36.2 us
    reduce_scatter x1, waiting for transfers between devices, shards(): lax.psum_scatter(jnp.dot(attn, out_proj, preferred_element_type=jnp.float...  25.9 us
    dot_general x3, matrix products, grad(): out = jnp.einsum('tf,td->fd', left, right, preferred_element_type=f32)  16.7 us
    all_gather x1, blocking collectives, shards(): key_piece = lax.all_gather(key_mine, 'ctx', axis=0, tiled=True)  15.7 us
    all_gather x1, blocking collectives, shards(): value_piece = lax.all_gather(value_mine, 'ctx', axis=0, tiled=True)  14 us
    dot_general x1, matrix products, shards(): up_val = jnp.einsum('td,fd->tf', rows, up_w, preferred_element_type=f32)  7.58 us
  transfers between devices with their start and end apart: 4, of which 3 were waited for; matrix products, arithmetic and copies ran while one was open for 13% of the time, Pallas kernels for 0%

profile of v1, /device:TPU:0, one launch (start us, length us, event | category | flops | bytes accessed | tf_op | source)
XLA Modules:
  0.0 352.9 jit_solution(4410886213488706627)
XLA Ops:
  7.2 0.0 copy-start
  7.2 0.0 reduce-scatter.3.cloned.1.call-start
  7.2 0.1 iota_compare_fusion
  7.4 0.7 constant_dynamic-slice_fusion.2
  8.1 15.7 %all_gather.15 = bf16[512,128]{1,0:T(8,128)(2,1)S(1)} all-gather(bf16[64,128]{1,0:T(8,128)(2,1)S(1)} %constant_dynamic-slice_fusion.2), channel_id=1, replica_groups=mesh['ctx'=8,'tp'=4] {'ctx'}, dimensions={0}, use_global_device_ids=true | all-gather | bytes 147456 | tf_op jit(solution)/shard_map/all_gather | solution.py:41
  23.8 0.4 select_reduce_fusion
  24.2 0.7 constant_dynamic-slice_fusion.1
  24.9 14.0 %all_gather.16 = bf16[512,128]{1,0:T(8,128)(2,1)S(1)} all-gather(bf16[64,128]{1,0:T(8,128)(2,1)S(1)} %constant_dynamic-slice_fusion.1), channel_id=1, replica_groups=mesh['ctx'=8,'tp'=4] {'ctx'}, dimensions={0}, use_global_device_ids=true | all-gather | bytes 147456 | tf_op jit(solution)/shard_map/all_gather | solution.py:42
  38.9 0.3 fusion.5
  39.2 0.4 fusion.4
  39.6 0.0 copy-start.2
  39.6 0.0 copy-start.4
  39.6 0.0 copy-start.5
  39.6 0.0 copy-start.6
  39.6 5.9 %convolution_convert_fusion.4 = bf16[64,4096]{1,0:T(8,128)(2,1)} fusion(bf16[1024,4096]{1,0:T(8,128)(2,1)} %param.16, bf16[8,8,8,128]{3,2,1,0:T(8,128)(2,1)S(1)} %fusion.4), kind=kOutput, calls=%fused_computation.4 | convolution fusion | flops 537133056 | bytes 9043968 | tf_op jit(solution)/shard_map/dot_general | solution.py:60
  45.5 0.0 reduce-scatter.3.cloned.1.call-update
  45.5 0.0 all-gather.3.cloned.1.call-start
  45.6 25.9 %reduce-scatter.3.cloned.1.call-done = bf16[16,4096]{1,0:T(8,128)(2,1)} async-done(((bf16[64,4096]{1,0:T(8,128)(2,1)}), bf16[16,4096]{1,0:T(8,128)(2,1)}) %reduce-scatter.3.cloned.1.call-update) | async-done | bytes 131088 | tf_op jit(solution)/shard_map/reduce_scatter | solution.py:59
  71.5 1.1 multiply_reduce_fusion
  72.5 1.7 multiply_convert_fusion.5
  74.2 0.0 all-gather.3.cloned.1.call-update
  74.2 0.0 all-gather.5.cloned.1.call-start
  74.3 0.7 all-gather.5.cloned.1.call-update
  74.9 0.0 reduce-scatter.5.cloned.1.call-start
  75.0 0.1 copy.26
  75.1 0.1 copy.25
  75.2 0.1 select_reduce_fusion.1
  75.3 69.0 %all_gather.18 = f32[512,16]{1,0:T(8,128)S(1)} all-gather(f32[16,16]{1,0:T(8,128)S(1)} %select_reduce_fusion.1), channel_id=1, replica_groups=mesh['ctx'=8,'tp'=4] {'ctx','tp'}, dimensions={0}, use_global_device_ids=true | all-gather | bytes 33792 | tf_op jit(solution)/shard_map/all_gather | solution.py:74
  144.3 0.1 constant_dynamic-slice_fusion
  144.4 0.6 broadcast_in_dim.51
  145.0 0.1 copy.29
  145.1 0.0 all-gather.3.cloned.1.call-done
  145.1 0.0 copy-start.7
  145.2 0.0 slice-start
  145.2 7.5 %fusion.22 = f32[512,768]{1,0:T(8,128)S(1)} fusion(bf16[512,4096]{1,0:T(8,128)(2,1)} %all-gather.3.cloned.1.call-done, bf16[768,4096]{1,0:T(8,128)(2,1)} %bitcast.58), kind=kOutput, calls=%fused_computation.47 | convolution fusion | flops 3221225472 | bytes 12058624 | tf_op jit(solution)/shard_map/td,fd->tf/dot_general | solution.py:87
  152.7 0.0 slice-start.1
  152.7 7.6 %multiply_convert_fusion.2 = (bf16[512,768]{1,0:T(8,128)(2,1)S(1)}, f32[512,768]{1,0:T(8,128)}) fusion(f32[512,768]{1,0:T(8,128)S(1)} %bitcast.55, f32[512,768]{1,0:T(8,128)S(1)} %fusion.22, bf16[512,4096]{1,0:T(8,128)(2,1)S(1)} %copy-done.7, bf16[768,4096]{1,0:T(8,128)(2,1)} %bitcast.59), kind=kOutput, calls=%fused_computation.7 | convolution fusion | flops 3223977984 | bytes 15990784 | tf_op jit(solution)/shard_map/td,fd->tf/dot_general | solution.py:88
  160.3 0.9 copy-done.11
  161.2 0.0 slice-done.1
  161.2 5.0 %convolution_convert_fusion.3 = bf16[512,4096]{1,0:T(8,128)(2,1)} fusion(bf16[512,768]{1,0:T(8,128)(2,1)S(1)} %get-tuple-element.6, bf16[768,4096]{1,0:T(8,128)(2,1)S(1)} %bitcast.63), kind=kOutput, calls=%fused_computation.3 | convolution fusion | flops 3223322624 | bytes 11272192 | tf_op jit(solution)/shard_map/dot_general | solution.py:92
  166.1 0.0 reduce-scatter.5.cloned.1.call-update
  166.2 36.2 %all-gather.5.cloned.1.call-done = bf16[512,4096]{1,0:T(8,128)(2,1)} async-done(((bf16[16,4096]{1,0:T(8,128)(2,1)}), bf16[512,4096]{1,0:T(8,128)(2,1)}) %all-gather.5.cloned.1.call-update) | async-done | bytes 4194320 | tf_op jit(solution)/shard_map/all_gather | solution.py:79
  202.3 7.3 %convolution_multiply_fusion = f32[512,768]{1,0:T(8,128)S(1)} fusion(f32[512,768]{1,0:T(8,128)S(1)} %bitcast.56, bf16[512,4096]{1,0:T(8,128)(2,1)} %all-gather.5.cloned.1.call-done, bf16[768,4096]{1,0:T(8,128)(2,1)} %bitcast.60), kind=kOutput, calls=%fused_computation.10 | convolution fusion | flops 3221618688 | bytes 13631488 | tf_op jit(solution)/shard_map/td,fd->tf/dot_general | solution.py:86
  209.6 5.4 %convolution_convert_fusion = bf16[768,4096]{1,0:T(8,128)(2,1)} fusion(bf16[512,768]{1,0:T(8,128)(2,1)S(1)} %copy-done.12, bf16[512,4096]{1,0:T(8,128)(2,1)S(1)} %copy-done.9), kind=kOutput, calls=%fused_computation | convolution fusion | flops 3224371200 | bytes 11272192 | tf_op jit(solution)/shard_map/tf,td->fd/dot_general | solution.py:100
  215.0 5.4 %convolution_convert_fusion.1 = bf16[768,4096]{1,0:T(8,128)(2,1)} fusion(bf16[512,4096]{1,0:T(8,128)(2,1)S(1)} %copy-done.8, f32[512,768]{1,0:T(8,128)S(1)} %convolution_multiply_fusion, f32[512,768]{1,0:T(8,128)S(1)} %fusion.22), kind=kOutput, calls=%fused_computation.1 | convolution fusion | flops 3226730496 | bytes 13631488 | tf_op jit(solution)/shard_map/tf,td->fd/dot_general | solution.py:100
  220.4 5.9 %convolution_convert_fusion.2 = bf16[768,4096]{1,0:T(8,128)(2,1)} fusion(bf16[512,4096]{1,0:T(8,128)(2,1)S(1)} %copy-done.8, f32[512,768]{1,0:T(8,128)S(1)} %fusion.22, f32[512,768]{1,0:T(8,128)S(1)} %convolution_multiply_fusion, f32[512,768]{1,0:T(8,128)S(1)} %copy-done.10), kind=kOutput, calls=%fused_computation.2 | convolution fusion | flops 3228303360 | bytes 15204352 | tf_op jit(solution)/shard_map/tf,td->fd/dot_general | solution.py:100
  226.4 118.4 %reduce-scatter.5.cloned.1.call-done = bf16[16,4096]{1,0:T(8,128)(2,1)} async-done(((bf16[512,4096]{1,0:T(8,128)(2,1)}), bf16[16,4096]{1,0:T(8,128)(2,1)}) %reduce-scatter.5.cloned.1.call-update) | async-done | bytes 131088 | tf_op jit(solution)/shard_map/reduce_scatter | solution.py:93
  344.8 1.6 add_convert_fusion
  (24 shorter events, 0.1 us)
Async XLA Ops:
  7.2 16.6 %copy-start = (bf16[64,1024]{1,0:T(8,128)(2,1)S(1)}, bf16[64,1024]{1,0:T(8,128)(2,1)}, u32[]{:S(2)}) copy-start(bf16[64,1024]{1,0:T(8,128)(2,1)} %param.12) | copy-start | bytes 393220
  7.2 64.3 %reduce-scatter.3.cloned.1.call-start = ((), (), s32[]{:S(2)}) async-start(), calls=%async_computation.2 | async-start | bytes 655360 | tf_op jit(solution)/shard_map/reduce_scatter | solution.py:59
  39.6 31.9 %copy-start.2 = (bf16[16,4096]{1,0:T(8,128)(2,1)S(1)}, bf16[16,4096]{1,0:T(8,128)(2,1)}, u32[]{:S(2)}) copy-start(bf16[16,4096]{1,0:T(8,128)(2,1)} %param.15) | copy-start | bytes 393220
  39.6 32.9 %copy-start.4 = (f32[4096]{0:T(1024)S(1)}, f32[4096]{0:T(1024)}, u32[]{:S(2)}) copy-start(f32[4096]{0:T(1024)} %param.17) | copy-start | bytes 49156
  39.6 35.4 %copy-start.5 = (f32[16,8]{0,1:T(8,128)S(1)}, f32[16,8]{0,1:T(8,128)}, u32[]{:S(2)}) copy-start(f32[16,8]{0,1:T(8,128)} %param.19) | copy-start | bytes 1540
  39.6 35.5 %copy-start.6 = (s32[16,8]{0,1:T(8,128)S(1)}, s32[16,8]{0,1:T(8,128)}, u32[]{:S(2)}) copy-start(s32[16,8]{0,1:T(8,128)} %param.18) | copy-start | bytes 1540
  45.5 99.6 %all-gather.3.cloned.1.call-start = ((), (), s32[]{:S(2)}) async-start(), calls=%async_computation.3 | async-start | bytes 4325376 | tf_op jit(solution)/shard_map/all_gather | solution.py:80
  74.2 128.1 %all-gather.5.cloned.1.call-start = ((), (), s32[]{:S(2)}) async-start(), calls=%async_computation.5 | async-start | bytes 4325376 | tf_op jit(solution)/shard_map/all_gather | solution.py:79
  74.9 269.8 %reduce-scatter.5.cloned.1.call-start = ((), (), s32[]{:S(2)}) async-start(), calls=%async_computation.4 | async-start | bytes 4325376 | tf_op jit(solution)/shard_map/reduce_scatter | solution.py:93
  145.1 7.5 %copy-start.7 = (bf16[512,4096]{1,0:T(8,128)(2,1)S(1)}, bf16[512,4096]{1,0:T(8,128)(2,1)}, u32[]{:S(2)}) copy-start(bf16[512,4096]{1,0:T(8,128)(2,1)} %all-gather.3.cloned.1.call-done) | copy-start | bytes 12582916
  145.2 16.0 %slice-start = ((s8[6291456]{0:T(1024)(128)(4,1)}), s8[4194304]{0:T(1024)(128)(4,1)S(1)}, s32[]{:S(2)}) async-start(s8[6291456]{0:T(1024)(128)(4,1)} %bitcast.61), calls=%async_computation.6 | async-start | bytes 8388608
  152.7 8.5 %slice-start.1 = ((s8[6291456]{0:T(1024)(128)(4,1)}), s8[2097152]{0:T(1024)(128)(4,1)S(1)}, s32[]{:S(2)}) async-start(s8[6291456]{0:T(1024)(128)(4,1)} %bitcast.61), calls=%async_computation.7 | async-start | bytes 4194304
  160.3 0.9 copy-start.11
  202.3 7.3 %copy-start.9 = (bf16[512,4096]{1,0:T(8,128)(2,1)S(1)}, bf16[512,4096]{1,0:T(8,128)(2,1)}, u32[]{:S(2)}) copy-start(bf16[512,4096]{1,0:T(8,128)(2,1)} %all-gather.5.cloned.1.call-done) | copy-start | bytes 12582916
  202.3 7.3 %copy-start.12 = (bf16[512,768]{1,0:T(8,128)(2,1)S(1)}, bf16[512,768]{1,0:T(8,128)(2,1)}, u32[]{:S(2)}) copy-start(bf16[512,768]{1,0:T(8,128)(2,1)} %copy-done.11) | copy-start | bytes 2359300
  209.6 5.4 %copy-start.8 = (bf16[512,4096]{1,0:T(8,128)(2,1)S(1)}, bf16[512,4096]{1,0:T(8,128)(2,1)}, u32[]{:S(2)}) copy-start(bf16[512,4096]{1,0:T(8,128)(2,1)} %all-gather.3.cloned.1.call-done) | copy-start | bytes 12582916
  215.0 5.4 %copy-start.10 = (f32[512,768]{1,0:T(8,128)S(1)}, f32[512,768]{1,0:T(8,128)}, u32[]{:S(2)}) copy-start(f32[512,768]{1,0:T(8,128)} %get-tuple-element.7) | copy-start | bytes 4718596
  220.4 124.4 %copy-start.3 = (bf16[16,4096]{1,0:T(8,128)(2,1)S(1)}, bf16[16,4096]{1,0:T(8,128)(2,1)}, u32[]{:S(2)}) copy-start(bf16[16,4096]{1,0:T(8,128)(2,1)} %reduce-scatter.3.cloned.1.call-done) | copy-start | bytes 393220
  220.4 126.0 %copy-start.1 = (bf16[64,1024]{1,0:T(8,128)(2,1)S(1)}, bf16[64,1024]{1,0:T(8,128)(2,1)}, u32[]{:S(2)}) copy-start(bf16[64,1024]{1,0:T(8,128)(2,1)} %param.12) | copy-start | bytes 393220
Sparse Core Ops, SparseCore 0:
  45.6 25.7 reduce-scatter.2
  75.3 62.6 all-gather.2
  141.3 60.9 all-gather.4
  204.6 140.1 reduce-scatter.4
